TPU v7x, 32 devices: a whole 2x2x4 slice. The times are simulated.
32 devices in a mesh: section: 4 (over z), tp: 8 (over y, x, core).
Axes of the slice: x: 2, y: 2, z: 4, core: 2. Of those that a mesh axis runs over, the one named last changes fastest.
Arguments:
- stash: bfloat16 [4, 4, 192, 1024], P('section', None, 'tp'), may hold values from -6 to 6
- w_in: bfloat16 [4, 1024, 65536], P('section', None, 'tp'), may hold values from -0.1875 to 0.1875
- w_out: bfloat16 [4, 65536, 1024], P('section', 'tp'), may hold values from -0.0234375 to 0.0234375
- gain: float32 [4, 1024], P('section'), may hold values from 0.1 to 1.9
- plan: int32 [3, 4], replicated, may hold values from 0 to 3
- arriving: bfloat16 [4, 192, 1024], P('section', 'tp'), may hold values from -6 to 6
- fresh: bfloat16 [2, 192, 1024], P(None, 'tp'), may hold values from -6 to 6
Outputs:
- input_grads: bfloat16 [3, 4, 192, 1024], P(None, 'section', 'tp')
All inputs are finite; a program needn't handle non-finite values.
Results may differ from a plain program's by a relative error of at most 0.0085.
Values may be sent and summed in bfloat16 or wider, within the bound.
No kernel may reach another device: no remote copies, remote signals or barrier semaphores. Data moves between devices by JAX's collectives and lax.ppermute only.
A program may use at most 128 MiB of HBM per device.

v0:
```python
import jax
import jax.numpy as jnp
from jax import lax
from jax.sharding import PartitionSpec as P

epsilon = 1e-06
contract_last = (((1,), (1,)), ((), ()))


def from_partner(value, axis, apart):
    return lax.ppermute(value, axis, [(i, i ^ 1 << apart) for i in range(lax.axis_size(axis))])


def shifted(value, axis, steps):
    count = lax.axis_size(axis)
    first, last = (max(0, -steps), min(count, count - steps))
    return lax.ppermute(value, axis, [(source, source + steps) for source in range(first, last)])


def norm_parts(x_rows):
    values = x_rows.astype(jnp.float32)
    inverse_rms = lax.rsqrt(jnp.mean(values * values, axis=-1, keepdims=True) + epsilon)
    return (inverse_rms, values * inverse_rms)


def norm_back(normed_grad, incoming, inverse_rms, normed, gain_row):
    scaled = normed_grad * gain_row
    inner = jnp.mean(scaled * normed, axis=-1, keepdims=True)
    return (incoming.astype(jnp.float32) + inverse_rms * (scaled - normed * inner)).astype(
        jnp.bfloat16
    )


def body(stash, w_in, w_out, gain, plan, arriving, fresh):
    section_index = lax.axis_index("section")
    section_total = lax.axis_size("section")
    half_bit = section_total.bit_length() - 2
    tp_index = lax.axis_index("tp")
    stored = stash[0]
    weight_in = w_in[0]
    weight_out = w_out[0]
    gain_row = gain[0]
    row_count = stored.shape[1]
    ticks = plan.shape[0]
    partner = (section_index + section_total // 2) % section_total
    is_last = section_index == section_total - 1
    offset = tp_index * row_count
    incoming_shard = arriving[0]
    results = []
    for tick in range(ticks):
        slot_now = plan[tick, partner]
        picked = lax.dynamic_index_in_dim(stored, slot_now, 0, keepdims=False)
        own_rows = from_partner(picked, "section", half_bit)
        full_rows = lax.all_gather(own_rows, "tp", axis=0, tiled=True)
        inverse_rms, normed = norm_parts(full_rows)
        inputs = (normed * gain_row).astype(jnp.bfloat16)
        preact = jnp.dot(inputs, weight_in, preferred_element_type=jnp.float32)
        incoming = lax.all_gather(incoming_shard, "tp", axis=0, tiled=True)
        hidden_back = lax.dot_general(
            incoming, weight_out, contract_last, preferred_element_type=jnp.float32
        )
        hidden_grad = (hidden_back * (2.0 * jnp.maximum(preact, 0.0))).astype(jnp.bfloat16)
        normed_grad = lax.psum_scatter(
            lax.dot_general(
                hidden_grad, weight_in, contract_last, preferred_element_type=jnp.float32
            ),
            "tp",
            scatter_dimension=0,
            tiled=True,
        )
        own_rms = lax.dynamic_slice_in_dim(inverse_rms, offset, row_count, 0)
        own_normed = lax.dynamic_slice_in_dim(normed, offset, row_count, 0)
        outgoing = norm_back(normed_grad, incoming_shard, own_rms, own_normed, gain_row)
        results.append(outgoing)
        if tick + 1 < ticks:
            below = shifted(outgoing, "section", -1)
            incoming_shard = jnp.where(is_last, fresh[tick], below)
    return jnp.stack(results)[:, None]


def solution(mesh):
    placed = (
        P("section", None, "tp", None),
        P("section", None, "tp"),
        P("section", "tp", None),
        P("section", None),
        P(),
        P("section", "tp", None),
        P(None, "tp", None),
    )
    return jax.shard_map(
        body, mesh=mesh, in_specs=placed, out_specs=P(None, "section", "tp", None), check_vma=False
    )
```

profile of v0, /device:TPU:0, one launch (start us, length us, event | category | flops | bytes accessed | tf_op | source)
XLA Modules:
  0.0 270.2 jit_solution(16858990861311271106)
XLA Ops:
  6.5 1.5 constant_dynamic-slice_fusion.1
  13.7 0.9 dynamic-slice_bitcast_fusion.1
  14.6 4.1 %collective-permute-start = (bf16[24,1024]{1,0:T(8,128)(2,1)S(1)}, bf16[24,1024]{1,0:T(8,128)(2,1)S(1)}, u32[]{:S(2)}, u32[]{:S(2)}) collective-permute-start(bf16[24,1024]{1,0:T(8,128)(2,1)S(1)} %get-tuple-element.6), channel_id=1, source_target_pairs={{0,16},{8,24},{16,0},{24,8},{1,17},{9,25},{17,1},{25,9},{2,18},{10... | collective-permute-start | bytes 147464 | tf_op jit(solution)/shard_map/ppermute | solution.py:11
  18.7 9.8 %all-gather = bf16[1,192,1024]{2,1,0:T(8,128)(2,1)S(1)} all-gather(bf16[1,24,1024]{2,1,0:T(8,128)(2,1)} %param.12), channel_id=2, replica_groups=mesh['section'=4,'tp'=8] {'tp'}, dimensions={1}, use_global_device_ids=true | all-gather | bytes 442368 | tf_op jit(solution)/shard_map/all_gather | solution.py:58
  28.5 9.3 %all_gather.18 = bf16[192,1024]{1,0:T(8,128)(2,1)S(1)} all-gather(bf16[24,1024]{1,0:T(8,128)(2,1)S(1)} %collective-permute-done), channel_id=1, replica_groups=mesh['section'=4,'tp'=8] {'tp'}, dimensions={0}, use_global_device_ids=true | all-gather | bytes 442368 | tf_op jit(solution)/shard_map/all_gather | solution.py:54
  37.8 0.2 fusion.60
  37.9 12.0 %fusion.33 = f32[192,8192]{1,0:T(8,128)} fusion(bf16[1,1024,8192]{2,1,0:T(8,128)(2,1)} %param.8, f32[1024]{0:T(1024)} %bitcast.83, bf16[192,1024]{1,0:T(8,128)(2,1)S(1)} %all_gather.18, f32[192]{0:T(256)S(1)} %add_rsqrt_fusion.2), kind=kOutput, calls=%fused_computation.23 | convolution fusion | flops 3225157632 | bytes 23466752 | tf_op jit(solution)/shard_map/dot_general | solution.py:57
  49.9 18.3 %fusion.8 = f32[192,1024]{1,0:T(8,128)} fusion(bf16[1,1024,8192]{2,1,0:T(8,128)(2,1)} %param.8, f32[192,8192]{1,0:T(8,128)} %fusion.33, bf16[1,8192,1024]{2,1,0:T(8,128)(2,1)} %param.9, bf16[1,192,1024]{2,1,0:T(8,128)(2,1)S(1)} %all-gather), kind=kOutput, calls=%fused_computation.8 | convolution fusion | flops 6445596672 | bytes 41025536 | tf_op jit(solution)/shard_map/dot_general | solution.py:64
  68.4 0.4 collective-permute-start.2
  68.9 5.6 %collective-permute-done.2 = bf16[24,1024]{1,0:T(8,128)(2,1)S(1)} collective-permute-done((bf16[24,1024]{1,0:T(8,128)(2,1)S(1)}, bf16[24,1024]{1,0:T(8,128)(2,1)S(1)}, u32[]{:S(2)}, u32[]{:S(2)}) %collective-permute-start.2) | collective-permute-done | bytes 49184 | tf_op jit(solution)/shard_map/ppermute | solution.py:11
  74.5 8.8 %all_gather.20 = bf16[192,1024]{1,0:T(8,128)(2,1)S(1)} all-gather(bf16[24,1024]{1,0:T(8,128)(2,1)S(1)} %collective-permute-done.2), channel_id=1, replica_groups=mesh['section'=4,'tp'=8] {'tp'}, dimensions={0}, use_global_device_ids=true | all-gather | bytes 442368 | tf_op jit(solution)/shard_map/all_gather | solution.py:54
  83.6 18.1 %reduce-scatter.4.cloned.1.call-done = f32[24,1024]{1,0:T(8,128)} async-done(((f32[192,1024]{1,0:T(8,128)}), f32[24,1024]{1,0:T(8,128)}) %reduce-scatter.4.cloned.1.call-update) | async-done | bytes 98320 | tf_op jit(solution)/shard_map/reduce_scatter | solution.py:63
  101.7 1.0 multiply_reduce_fusion.2
  102.7 1.0 fusion.68
  103.7 1.4 collective-permute-start.1
  105.2 12.0 %fusion.30 = f32[192,8192]{1,0:T(8,128)} fusion(bf16[1,1024,8192]{2,1,0:T(8,128)(2,1)} %param.8, f32[1024]{0:T(1024)S(1)} %bitcast.86, bf16[192,1024]{1,0:T(8,128)(2,1)S(1)} %all_gather.20, f32[192]{0:T(256)S(1)} %add_rsqrt_fusion.1), kind=kOutput, calls=%fused_computation.22 | convolution fusion | flops 3225157632 | bytes 23466752 | tf_op jit(solution)/shard_map/dot_general | solution.py:57
  117.2 9.7 %all_gather.21 = bf16[192,1024]{1,0:T(8,128)(2,1)S(1)} all-gather(bf16[24,1024]{1,0:T(8,128)(2,1)S(1)} %bitcast_select_fusion.1), channel_id=1, replica_groups=mesh['section'=4,'tp'=8] {'tp'}, dimensions={0}, use_global_device_ids=true | all-gather | bytes 442368 | tf_op jit(solution)/shard_map/all_gather | solution.py:58
  126.9 18.3 %fusion.4 = f32[192,1024]{1,0:T(8,128)} fusion(bf16[1,1024,8192]{2,1,0:T(8,128)(2,1)} %param.8, f32[192,8192]{1,0:T(8,128)} %fusion.30, bf16[192,1024]{1,0:T(8,128)(2,1)S(1)} %all_gather.21, bf16[1,8192,1024]{2,1,0:T(8,128)(2,1)} %param.9), kind=kOutput, calls=%fused_computation.4 | convolution fusion | flops 6445596672 | bytes 41025536 | tf_op jit(solution)/shard_map/dot_general | solution.py:64
  145.3 3.6 %collective-permute-start.4 = (bf16[24,1024]{1,0:T(8,128)(2,1)S(1)}, bf16[24,1024]{1,0:T(8,128)(2,1)S(1)}, u32[]{:S(2)}, u32[]{:S(2)}) collective-permute-start(bf16[24,1024]{1,0:T(8,128)(2,1)S(1)} %get-tuple-element.7), channel_id=1, source_target_pairs={{0,16},{8,24},{16,0},{24,8},{1,17},{9,25},{17,1},{25,9},{2,18},{10... | collective-permute-start | bytes 147464 | tf_op jit(solution)/shard_map/ppermute | solution.py:11
  149.0 2.2 collective-permute-done.4
  151.2 8.7 %all_gather.22 = bf16[192,1024]{1,0:T(8,128)(2,1)S(1)} all-gather(bf16[24,1024]{1,0:T(8,128)(2,1)S(1)} %collective-permute-done.4), channel_id=1, replica_groups=mesh['section'=4,'tp'=8] {'tp'}, dimensions={0}, use_global_device_ids=true | all-gather | bytes 442368 | tf_op jit(solution)/shard_map/all_gather | solution.py:54
  160.1 21.4 %reduce-scatter.6.cloned.1.call-done = f32[24,1024]{1,0:T(8,128)} async-done(((f32[192,1024]{1,0:T(8,128)}), f32[24,1024]{1,0:T(8,128)}) %reduce-scatter.6.cloned.1.call-update) | async-done | bytes 98320 | tf_op jit(solution)/shard_map/reduce_scatter | solution.py:63
  181.5 1.0 multiply_reduce_fusion.1
  182.6 1.0 add_convert_fusion.1
  183.5 1.3 collective-permute-start.3
  184.8 12.0 %fusion.27 = f32[192,8192]{1,0:T(8,128)} fusion(bf16[1,1024,8192]{2,1,0:T(8,128)(2,1)} %param.8, f32[1024]{0:T(1024)S(1)} %bitcast.89, bf16[192,1024]{1,0:T(8,128)(2,1)S(1)} %all_gather.22, f32[192]{0:T(256)S(1)} %add_rsqrt_fusion), kind=kOutput, calls=%fused_computation.21 | convolution fusion | flops 3225157632 | bytes 23466752 | tf_op jit(solution)/shard_map/dot_general | solution.py:57
  196.8 9.5 %all_gather.23 = bf16[192,1024]{1,0:T(8,128)(2,1)S(1)} all-gather(bf16[24,1024]{1,0:T(8,128)(2,1)S(1)} %bitcast_select_fusion), channel_id=1, replica_groups=mesh['section'=4,'tp'=8] {'tp'}, dimensions={0}, use_global_device_ids=true | all-gather | bytes 442368 | tf_op jit(solution)/shard_map/all_gather | solution.py:58
  206.4 18.3 %fusion = f32[192,1024]{1,0:T(8,128)} fusion(bf16[1,1024,8192]{2,1,0:T(8,128)(2,1)} %param.8, f32[192,8192]{1,0:T(8,128)} %fusion.27, bf16[192,1024]{1,0:T(8,128)(2,1)S(1)} %all_gather.23, bf16[1,8192,1024]{2,1,0:T(8,128)(2,1)} %param.9), kind=kOutput, calls=%fused_computation | convolution fusion | flops 6445596672 | bytes 41025536 | tf_op jit(solution)/shard_map/dot_general | solution.py:64
  224.9 36.1 %reduce-scatter.8.cloned.1.call-done = f32[24,1024]{1,0:T(8,128)} async-done(((f32[192,1024]{1,0:T(8,128)}), f32[24,1024]{1,0:T(8,128)}) %reduce-scatter.8.cloned.1.call-update) | async-done | bytes 98320 | tf_op jit(solution)/shard_map/reduce_scatter | solution.py:63
  261.0 1.0 multiply_reduce_fusion
  262.0 1.0 fusion.69
  263.0 0.7 maximum_bitcast_fusion
  (31 shorter events, 1.1 us)
Async XLA Ops:
  6.5 95.2 %reduce-scatter.4.cloned.1.call-start = ((), (), s32[]{:S(2)}) async-start(), calls=%async_computation.3 | async-start | bytes 884736 | tf_op jit(solution)/shard_map/reduce_scatter | solution.py:63
  14.6 13.9 %collective-permute-start = (bf16[24,1024]{1,0:T(8,128)(2,1)S(1)}, bf16[24,1024]{1,0:T(8,128)(2,1)S(1)}, u32[]{:S(2)}, u32[]{:S(2)}) collective-permute-start(bf16[24,1024]{1,0:T(8,128)(2,1)S(1)} %get-tuple-element.6), channel_id=1, source_target_pairs={{0,16},{8,24},{16,0},{24,8},{1,17},{9,25},{17,1},{25,9},{2,18},{10... | collective-permute-start | bytes 147464 | tf_op jit(solution)/shard_map/ppermute | solution.py:11
  49.9 51.8 %copy-start.1 = (f32[1,1024]{1,0:T(1,128)S(1)}, f32[1,1024]{1,0:T(1,128)}, u32[]{:S(2)}) copy-start(f32[1,1024]{1,0:T(1,128)} %param.10) | copy-start | bytes 12292
  49.9 52.8 %copy-start = (bf16[1,24,1024]{2,1,0:T(8,128)(2,1)S(1)}, bf16[1,24,1024]{2,1,0:T(8,128)(2,1)}, u32[]{:S(2)}) copy-start(bf16[1,24,1024]{2,1,0:T(8,128)(2,1)} %param.12) | copy-start | bytes 147460
  68.3 113.2 %reduce-scatter.6.cloned.1.call-start = ((), (), s32[]{:S(2)}) async-start(), calls=%async_computation.4 | async-start | bytes 884736 | tf_op jit(solution)/shard_map/reduce_scatter | solution.py:63
  68.4 6.1 %collective-permute-start.2 = (bf16[24,1024]{1,0:T(8,128)(2,1)S(1)}, bf16[24,1024]{1,0:T(8,128)(2,1)S(1)}, u32[]{:S(2)}, u32[]{:S(2)}) collective-permute-start(bf16[24,1024]{1,0:T(8,128)(2,1)S(1)} %get-tuple-element.5), channel_id=1, source_target_pairs={{0,16},{8,24},{16,0},{24,8},{1,17},{9,25},{17,1},{25,9},{2,18},{10... | collective-permute-start | bytes 147464 | tf_op jit(solution)/shard_map/ppermute | solution.py:11
  103.7 13.4 %copy-start.2 = (bf16[2,24,1024]{2,1,0:T(8,128)(2,1)S(1)}, bf16[2,24,1024]{2,1,0:T(8,128)(2,1)}, u32[]{:S(2)}) copy-start(bf16[2,24,1024]{2,1,0:T(8,128)(2,1)} %param.13) | copy-start | bytes 294916
  103.7 13.4 %collective-permute-start.1 = (bf16[24,1024]{1,0:T(8,128)(2,1)S(1)}, bf16[24,1024]{1,0:T(8,128)(2,1)S(1)}, u32[]{:S(2)}, u32[]{:S(2)}) collective-permute-start(bf16[24,1024]{1,0:T(8,128)(2,1)S(1)} %fusion.68), channel_id=1, source_target_pairs={{8,0},{16,8},{24,16},{9,1},{17,9},{25,17},{10,2},{18,10},{26,18},{... | collective-permute-start | bytes 147464 | tf_op jit(solution)/shard_map/ppermute | solution.py:17
  145.2 115.8 %reduce-scatter.8.cloned.1.call-start = ((), (), s32[]{:S(2)}) async-start(), calls=%async_computation.5 | async-start | bytes 884736 | tf_op jit(solution)/shard_map/reduce_scatter | solution.py:63
  145.3 5.9 %collective-permute-start.4 = (bf16[24,1024]{1,0:T(8,128)(2,1)S(1)}, bf16[24,1024]{1,0:T(8,128)(2,1)S(1)}, u32[]{:S(2)}, u32[]{:S(2)}) collective-permute-start(bf16[24,1024]{1,0:T(8,128)(2,1)S(1)} %get-tuple-element.7), channel_id=1, source_target_pairs={{0,16},{8,24},{16,0},{24,8},{1,17},{9,25},{17,1},{25,9},{2,18},{10... | collective-permute-start | bytes 147464 | tf_op jit(solution)/shard_map/ppermute | solution.py:11
  183.5 13.3 %collective-permute-start.3 = (bf16[24,1024]{1,0:T(8,128)(2,1)S(1)}, bf16[24,1024]{1,0:T(8,128)(2,1)S(1)}, u32[]{:S(2)}, u32[]{:S(2)}) collective-permute-start(bf16[24,1024]{1,0:T(8,128)(2,1)S(1)} %add_convert_fusion.1), channel_id=1, source_target_pairs={{8,0},{16,8},{24,16},{9,1},{17,9},{25,17},{10,2},{18,10},{26,18},{... | collective-permute-start | bytes 147464 | tf_op jit(solution)/shard_map/ppermute | solution.py:17
Sparse Core Ops, SparseCore 0:
  68.4 33.2 reduce-scatter.3
  145.4 36.1 reduce-scatter.5
  224.8 36.1 reduce-scatter.7
where the time goes:
time: 271 us; the launch traced here: 270 us
  matrix products  90.9 us (34%)
  waiting for transfers between devices  83.5 us (31%)
  blocking collectives  55.9 us (21%)
  between operations  18.9 us (7%)
  starting transfers between devices  10.9 us (4%)
  other arithmetic  7.59 us (3%)
    reduce_scatter x3, waiting for transfers between devices, body(): lax.psum_scatter(lax.dot_general(hidden_grad, weight_in, contract_last, p...  75.6 us
    dot_general x3, matrix products, body(): lax.dot_general(hidden_grad, weight_in, contract_last, preferred_element_...  55 us
    dot_general x3, matrix products, body(): preact = jnp.dot(inputs, weight_in, preferred_element_type=jnp.float32)  35.9 us
    all_gather x3, blocking collectives, body(): incoming = lax.all_gather(incoming_shard, 'tp', axis=0, tiled=True)  29.1 us
    all_gather x3, blocking collectives, body(): full_rows = lax.all_gather(own_rows, 'tp', axis=0, tiled=True)  26.8 us
    ppermute x3, starting transfers between devices, from_partner(): lax.ppermute(value, axis, [(i, i ^ 1 << apart) for i in range(lax.axis_si...  8.13 us
    ppermute x3, waiting for transfers between devices, from_partner(): lax.ppermute(value, axis, [(i, i ^ 1 << apart) for i in range(lax.axis_si...  7.8 us
  transfers between devices with their start and end apart: 8, of which 5 were waited for; matrix products, arithmetic and copies ran while one was open for 9% of the time, Pallas kernels for 0%

commit v1 on v0

v1 whole, which is shorter than its diff:
```python
import functools

import jax
import jax.numpy as jnp
from jax import lax
from jax.experimental import pallas as pl
from jax.experimental.pallas import tpu as pltpu
from jax.sharding import PartitionSpec as P

epsilon = 1e-06
MIB = 2**20
f32 = jnp.float32
bf16 = jnp.bfloat16
VMEM = pl.BlockSpec(memory_space=pltpu.VMEM)
HBM = pl.BlockSpec(memory_space=pltpu.HBM)
SMEM = pl.BlockSpec(memory_space=pltpu.SMEM)


def shape_of(shape, dtype):
    return jax.ShapeDtypeStruct(shape, dtype)


def limit(mib):
    return pltpu.CompilerParams(vmem_limit_bytes=mib * MIB)


def swapped(value, mask):
    return lax.ppermute(value, "tp", [(i, i ^ mask) for i in range(lax.axis_size("tp"))])


def from_mirror(value):
    count = lax.axis_size("section")
    return lax.ppermute(value, "section", [(i, (i + count // 2) % count) for i in range(count)])


def from_above(value, mask):
    sections, parts = lax.axis_size("section"), lax.axis_size("tp")
    pairs = [
        (((s + 1) % sections) * parts + (i ^ mask), s * parts + i)
        for s in range(sections)
        for i in range(parts)
    ]
    return lax.ppermute(value, ("section", "tp"), pairs)


def with_cores(chips):
    return chips + [swapped(value, 1) for value in chips]


def gathered(value):
    masks = range(2, lax.axis_size("tp"), 2)
    return with_cores([value] + [swapped(value, mask) for mask in masks])


def pick_kernel(plan, stash, first, later):
    sections = lax.axis_size("section")
    partner = lax.rem(lax.axis_index("section") + sections // 2, sections)
    first[...] = stash[0, plan[0, partner]]
    for tick in range(1, plan.shape[0]):
        later[tick - 1] = stash[0, plan[tick, partner]]


def pick(plan, stash):
    ticks, (_, _, rows, width) = plan.shape[0], stash.shape
    return pl.pallas_call(
        pick_kernel,
        out_shape=(
            shape_of((rows, width), stash.dtype),
            shape_of((ticks - 1, rows, width), stash.dtype),
        ),
        in_specs=[SMEM, VMEM],
        out_specs=(VMEM, VMEM),
        name="pick",
    )(plan, stash)


def joined(blocks):
    return jnp.concatenate([block[...].astype(f32) for block in blocks], axis=0)


def kernel_blocks(blocks):
    if blocks[0].shape[0] % 8 == 0:
        return list(blocks)
    return [jnp.concatenate(blocks, axis=0)]


def normalised(values):
    inverse_rms = lax.rsqrt(jnp.mean(values * values, axis=-1, keepdims=True) + epsilon)
    return inverse_rms, values * inverse_rms


def gate_kernel(count, *refs):
    blocks, (gain, w_in, out, inputs) = refs[:count], refs[count:]

    @pl.when(pl.program_id(0) == 0)
    def _():
        inputs[...] = (normalised(joined(blocks))[1] * gain[...]).astype(bf16)

    preact = jnp.dot(inputs[...], w_in[...], preferred_element_type=f32)
    out[...] = (2.0 * jnp.maximum(preact, 0.0)).T.astype(bf16)


def gate(blocks, gain, w_in, chunk):
    blocks = kernel_blocks(blocks)
    tokens = sum(block.shape[0] for block in blocks)
    width, hidden = w_in.shape
    chunk = min(chunk, hidden)
    return pl.pallas_call(
        functools.partial(gate_kernel, len(blocks)),
        out_shape=shape_of((hidden, tokens), bf16),
        grid=(hidden // chunk,),
        in_specs=[VMEM] * len(blocks) + [VMEM, pl.BlockSpec((width, chunk), lambda i: (0, i))],
        out_specs=pl.BlockSpec((chunk, tokens), lambda i: (i, 0)),
        scratch_shapes=[pltpu.VMEM((tokens, width), bf16)],
        compiler_params=limit(24),
        cost_estimate=pl.CostEstimate(
            flops=2 * tokens * width * hidden,
            bytes_accessed=2 * width * hidden + 2 * tokens * hidden,
            transcendentals=0,
        ),
        name="gate",
    )(*blocks, gain, w_in)


def back_kernel(count, chunk, *refs):
    blocks, (gates, w_out, w_in, own, other, gates_v, out_v, in_v, total, sems) = (
        refs[:count],
        refs[count:],
    )
    steps = gates.shape[0] // chunk
    copies = []
    for step in range(steps):
        part = pl.ds(step * chunk, chunk)
        copies.append(
            (
                pltpu.make_async_copy(w_out.at[part, :], out_v.at[part, :], sems.at[0, step]),
                pltpu.make_async_copy(gates.at[part, :], gates_v.at[part, :], sems.at[1, step]),
                pltpu.make_async_copy(w_in.at[:, part], in_v.at[:, part], sems.at[2, step]),
            )
        )
    for group in copies:
        for copy in group:
            copy.start()
    incoming = joined(blocks).T.astype(bf16)
    for step in range(steps):
        part = pl.ds(step * chunk, chunk)
        copies[step][0].wait()
        hidden_back = jnp.dot(out_v[part, :], incoming, preferred_element_type=f32)
        copies[step][1].wait()
        hidden_grad = (hidden_back * gates_v[part, :].astype(f32)).astype(bf16)
        copies[step][2].wait()
        partial = jnp.dot(in_v[:, part], hidden_grad, preferred_element_type=f32)
        if step == 0:
            total[...] = partial
        else:
            total[...] += partial
    sums = total[...].T
    half = own.shape[0]
    own[...] = sums[:half]
    other[...] = sums[half:].astype(bf16)


def back(blocks, gates, w_out, w_in, chunk):
    blocks = kernel_blocks(blocks)
    hidden, tokens = gates.shape
    width = w_in.shape[0]
    chunk = min(chunk, hidden)
    return pl.pallas_call(
        functools.partial(back_kernel, len(blocks), chunk),
        out_shape=(
            shape_of((tokens // 2, width), f32),
            shape_of((tokens // 2, width), bf16),
        ),
        in_specs=[VMEM] * len(blocks) + [HBM] * 3,
        out_specs=(VMEM, VMEM),
        scratch_shapes=[
            pltpu.VMEM((hidden, tokens), bf16),
            pltpu.VMEM((hidden, width), bf16),
            pltpu.VMEM((width, hidden), bf16),
            pltpu.VMEM((width, tokens), f32),
            pltpu.SemaphoreType.DMA((3, hidden // chunk)),
        ],
        compiler_params=limit(48),
        cost_estimate=pl.CostEstimate(
            flops=4 * tokens * width * hidden,
            bytes_accessed=4 * width * hidden + 2 * tokens * hidden,
            transcendentals=0,
        ),
        name="back",
    )(*blocks, gates, w_out, w_in)


def fold_values(own, received, rows):
    sums = own + received.astype(f32)
    return [sums[:rows]] + [
        sums[at : at + rows].astype(bf16) for at in range(rows, sums.shape[0], rows)
    ]


def fold_kernel(rows, own, received, *outs):
    for out, value in zip(outs, fold_values(own[...], received[...], rows)):
        out[...] = value


def fold(own, received, rows):
    if rows % 8:
        return fold_values(own, received, rows)
    half, width = own.shape
    return pl.pallas_call(
        functools.partial(fold_kernel, rows),
        out_shape=tuple(
            shape_of((rows, width), bf16 if at else f32) for at in range(half // rows)
        ),
        in_specs=[VMEM] * 2,
        out_specs=tuple([VMEM] * (half // rows)),
        name="fold",
    )(own, received)


def finish_kernel(ending, *refs):
    own, incoming, x_rows, gain, extra = refs[:5]
    received, outs = (refs[5:-1], refs[-1:]) if ending else (refs[5:-2], refs[-2:])
    if ending:
        past, received = received[:ending], received[ending:]
    total = own[...]
    for block in received:
        total = total + block[...].astype(f32)
    inverse_rms, normed = normalised(x_rows[...].astype(f32))
    scaled = total * gain[...]
    inner = jnp.mean(scaled * normed, axis=-1, keepdims=True)
    result = (incoming[...].astype(f32) + inverse_rms * (scaled - normed * inner)).astype(bf16)
    if ending:
        for tick in range(ending):
            outs[0][tick, 0] = past[tick][...]
        outs[0][ending, 0] = result
    else:
        outs[0][...] = result
        outs[1][...] = jnp.where(lax.axis_index("section") == 0, extra[...], result)


def finish(own, received, incoming, x_rows, gain, fresh, past=None):
    rows, width = own.shape
    ending = 0 if past is None else len(past)
    block = shape_of((rows, width), bf16)
    whole = shape_of((ending + 1, 1, rows, width), bf16)
    operands = [own, incoming, x_rows, gain, gain if ending else fresh]
    operands += (past if ending else []) + list(received)
    return pl.pallas_call(
        functools.partial(finish_kernel, ending),
        out_shape=whole if ending else (block, block),
        in_specs=[VMEM] * len(operands),
        out_specs=VMEM if ending else (VMEM, VMEM),
        name="finish",
    )(*operands)


def body(stash, w_in, w_out, gain, plan, arriving, fresh):
    ticks, rows = plan.shape[0], stash.shape[2]
    weight_in, weight_out = w_in[0], w_out[0]
    masks = range(2, lax.axis_size("tp"), 2)
    first, later = pick(plan, stash)
    incoming = gathered(arriving[0])
    x_now = gathered(from_mirror(first))
    x_later = gathered(from_mirror(later))
    gates = gate(x_now, gain, weight_in, 2048)
    results = []
    for tick in range(ticks):
        own, other = back(incoming, gates, weight_out, weight_in, 1024)
        blocks = fold(own, swapped(other, 1), rows)
        received = [swapped(block, mask) for block, mask in zip(blocks[1:], masks)]
        if tick + 1 == ticks:
            return finish(blocks[0], received, incoming[0], x_now[0], gain, None, results)
        result, outgoing = finish(
            blocks[0], received, incoming[0], x_now[0], gain, fresh[tick]
        )
        results.append(result)
        x_now = [block[tick] for block in x_later]
        gates = gate(x_now, gain, weight_in, 2048)
        incoming = with_cores([from_above(outgoing, mask) for mask in [0, *masks]])


def solution(mesh):
    placed = (
        P("section", None, "tp", None),
        P("section", None, "tp"),
        P("section", "tp", None),
        P("section", None),
        P(),
        P("section", "tp", None),
        P(None, "tp", None),
    )
    return jax.shard_map(
        body, mesh=mesh, in_specs=placed, out_specs=P(None, "section", "tp", None), check_vma=False
    )
```

time: 271 us -> 200 us (0.74)
  Pallas kernels: 0 us -> 98.1 us
  matrix products: 90.9 us -> 0 us
  waiting for transfers between devices: 83.5 us -> 26.7 us
  blocking collectives: 55.9 us -> 0 us
  starting transfers between devices: 10.9 us -> 46 us
  local copies, waits for them, and re-layouts: 2.59 us -> 25.6 us
  between operations: 18.9 us -> 0.54 us
  other arithmetic: 7.59 us -> 0 us
    pallas_call x0 -> x13, Pallas kernels: none -> 98.1 us  [the longest x3 68.7 us: back(): pl.pallas_call(functools.partial(back_kernel, len(blocks), chunk), out_sh...]
    dot_general x6 -> x0, matrix products: 90.9 us -> none  [the longest x3 55 us: body(): lax.dot_general(hidden_grad, weight_in, contract_last, preferred_element_...]
    reduce_scatter x3 -> x0, waiting for transfers between devices: 75.6 us -> none  [body(): lax.psum_scatter(lax.dot_general(hidden_grad, weight_in, contract_last, p...]
    all_gather x6 -> x0, blocking collectives: 55.9 us -> none  [the longest x3 29.1 us: body(): incoming = lax.all_gather(incoming_shard, 'tp', axis=0, tiled=True)]
    ppermute x5 -> x51, starting transfers between devices: 10.8 us -> 46 us  [the longest x41 27 us: swapped(): lax.ppermute(value, 'tp', [(i, i ^ mask) for i in range(lax.axis_size('tp...]
    unnamed x6 -> x54, local copies, waits for them, and re-layouts: 0.01 us -> 24.1 us
    ppermute x5 -> x51, waiting for transfers between devices: 7.8 us -> 26.7 us  [the longest x41 17.6 us: swapped(): lax.ppermute(value, 'tp', [(i, i ^ mask) for i in range(lax.axis_size('tp...]
    reduce_sum x6 -> x0, other arithmetic: 3.52 us -> none  [the longest x3 3.05 us: norm_back(): inner = jnp.mean(scaled * normed, axis=-1, keepdims=True)]
  transfers between devices with their start and end apart: 8 -> 51, of which waited for: 5 -> 20; matrix products, arithmetic and copies ran while one was open for 9% -> 1% of each run, Pallas kernels for 0% -> 22%
where the time goes in v1:
time: 200 us; the launch traced here: 197 us
  Pallas kernels  98.1 us (49%)
  starting transfers between devices  46 us (23%)
  waiting for transfers between devices  26.7 us (13%)
  local copies, waits for them, and re-layouts  25.6 us (13%)
    pallas_call x3, Pallas kernels, back(): pl.pallas_call(functools.partial(back_kernel, len(blocks), chunk), out_sh...  68.7 us
    ppermute x41, starting transfers between devices, swapped(): lax.ppermute(value, 'tp', [(i, i ^ mask) for i in range(lax.axis_size('tp...  27 us
    unnamed x54, local copies, waits for them, and re-layouts  24.1 us
    ppermute x41, waiting for transfers between devices, swapped(): lax.ppermute(value, 'tp', [(i, i ^ mask) for i in range(lax.axis_size('tp...  17.6 us
    pallas_call x3, Pallas kernels, gate(): pl.pallas_call(functools.partial(gate_kernel, len(blocks)), out_shape=sha...  17.1 us
    ppermute x8, starting transfers between devices, from_above(): return lax.ppermute(value, ('section', 'tp'), pairs)  14.6 us
    ppermute x8, waiting for transfers between devices, from_above(): return lax.ppermute(value, ('section', 'tp'), pairs)  9.12 us
    pallas_call x3, Pallas kernels, finish(): pl.pallas_call(functools.partial(finish_kernel, ending), out_shape=whole...  5.52 us
  transfers between devices with their start and end apart: 51, of which 20 were waited for; matrix products, arithmetic and copies ran while one was open for 1% of the time, Pallas kernels for 22%

profile of v1, /device:TPU:0, one launch (start us, length us, event | category | flops | bytes accessed | tf_op | source)
XLA Modules:
  0.0 197.0 jit_solution(17794011389848601233)
XLA Ops:
  0.0 1.6 pick.1
  1.6 4.0 %collective-permute-start.7 = (bf16[24,1024]{1,0:T(8,128)(2,1)}, bf16[24,1024]{1,0:T(8,128)(2,1)S(1)}, u32[]{:S(2)}, u32[]{:S(2)}) collective-permute-start(bf16[24,1024]{1,0:T(8,128)(2,1)} %get-tuple-element.29), channel_id=1, source_target_pairs={{0,16},{8,24},{16,0},{24,8},{1,17},{9,25},{17,1},{25,9},{2,18},{10... | collective-permute-start | bytes 147464 | tf_op jit(solution)/shard_map/ppermute | solution.py:33
  7.1 1.5 collective-permute-start.1
  14.3 1.8 collective-permute-start.2
  17.6 1.9 collective-permute-done.2.refs_3_
  20.5 1.8 collective-permute-start.30
  22.3 5.8 %copy-done = bf16[1,1024,8192]{2,1,0:T(8,128)(2,1)S(1)} copy-done((bf16[1,1024,8192]{2,1,0:T(8,128)(2,1)S(1)}, bf16[1,1024,8192]{2,1,0:T(8,128)(2,1)}, u32[]{:S(2)}) %copy-start) | copy-done | bytes 16777240
  28.8 5.7 %gate.3.refs_8_ = bf16[8192,192]{1,0:T(8,128)(2,1)S(1)} custom-call(bf16[24,1024]{1,0:T(8,128)(2,1)S(1)} %collective-permute-done.7.refs_0_.refs_2_, bf16[24,1024]{1,0:T(8,128)(2,1)S(1)} %collective-permute-done.8.refs_1_, bf16[24,1024]{1,0:T(8,128)(2,1)S(1)} %collective-permute-done.9.refs_2_, bf16[24,1024]{1,0:T(8,128)(2,1)S(1)} %collective-permute-done.10.refs_3_, ...), custom_call_target="tpu_custom_call" | custom-call | flops 3221225472 | bytes 19922944 | tf_op jit(solution)/shard_map/gate/pallas_call | solution.py:108
  36.3 22.9 %back.3 = (f32[96,1024]{1,0:T(8,128)S(1)}, bf16[96,1024]{1,0:T(8,128)(2,1)S(1)}) custom-call(bf16[24,1024]{1,0:T(8,128)(2,1)S(1)} %bitcast.50, bf16[24,1024]{1,0:T(8,128)(2,1)S(1)} %collective-permute-done.refs_1_, bf16[24,1024]{1,0:T(8,128)(2,1)S(1)} %collective-permute-done.1.refs_2_, bf16[24,1024]{1,0:T(8,128)(2,1)S(1)} %collective-permute-done.2.refs_3_, ...), custom_call_target="tpu_custom_call" | custom-call | flops 6442450944 | bytes 36700160 | tf_op jit(solution)/shard_map/back/pallas_call | solution.py:168
  62.4 1.7 fold.3
  65.0 1.5 collective-permute-start.17
  69.3 2.4 %collective-permute-done.18.refs_7_ = bf16[24,1024]{1,0:T(8,128)(2,1)S(1)} collective-permute-done((bf16[24,1024]{1,0:T(8,128)(2,1)}, bf16[24,1024]{1,0:T(8,128)(2,1)S(1)}, u32[]{:S(2)}, u32[]{:S(2)}) %collective-permute-start.18) | collective-permute-done | bytes 49184 | tf_op jit(solution)/shard_map/ppermute | solution.py:28
  72.4 1.8 finish.3
  74.2 5.7 %collective-permute-start.19 = (bf16[24,1024]{1,0:T(8,128)(2,1)}, bf16[24,1024]{1,0:T(8,128)(2,1)S(1)}, u32[]{:S(2)}, u32[]{:S(2)}) collective-permute-start(bf16[24,1024]{1,0:T(8,128)(2,1)} %get-tuple-element.36), channel_id=1, source_target_pairs={{8,0},{9,1},{10,2},{11,3},{12,4},{13,5},{14,6},{15,7},{16,8},{17,9... | collective-permute-start | bytes 147464 | tf_op jit(solution)/shard_map/ppermute | solution.py:43
  80.4 1.5 collective-permute-start.22
  82.0 3.1 %collective-permute-done.20.refs_1_ = bf16[24,1024]{1,0:T(8,128)(2,1)S(1)} collective-permute-done((bf16[24,1024]{1,0:T(8,128)(2,1)}, bf16[24,1024]{1,0:T(8,128)(2,1)S(1)}, u32[]{:S(2)}, u32[]{:S(2)}) %collective-permute-start.20) | collective-permute-done | bytes 49184 | tf_op jit(solution)/shard_map/ppermute | solution.py:43
  86.6 5.8 %copy-done.1 = bf16[1,1024,8192]{2,1,0:T(8,128)(2,1)S(1)} copy-done((bf16[1,1024,8192]{2,1,0:T(8,128)(2,1)S(1)}, bf16[1,1024,8192]{2,1,0:T(8,128)(2,1)}, u32[]{:S(2)}) %copy-start.1) | copy-done | bytes 16777240
  92.3 5.7 %gate.4.refs_8_ = bf16[8192,192]{1,0:T(8,128)(2,1)S(1)} custom-call(bf16[24,1024]{1,0:T(8,128)(2,1)S(1)} %get-tuple-element.68.refs_0_.refs_2_, bf16[24,1024]{1,0:T(8,128)(2,1)S(1)} %get-tuple-element.66.refs_1_, bf16[24,1024]{1,0:T(8,128)(2,1)S(1)} %get-tuple-element.64.refs_2_, bf16[24,1024]{1,0:T(8,128)(2,1)S(1)} %get-tuple-element.62.refs_3_, ...), custom_call_target="tpu_custom_call" | custom-call | flops 3221225472 | bytes 19922944 | tf_op jit(solution)/shard_map/gate/pallas_call | solution.py:108
  98.1 22.9 %back.4 = (f32[96,1024]{1,0:T(8,128)S(1)}, bf16[96,1024]{1,0:T(8,128)(2,1)S(1)}) custom-call(bf16[24,1024]{1,0:T(8,128)(2,1)S(1)} %collective-permute-done.19.refs_0_.refs_1_, bf16[24,1024]{1,0:T(8,128)(2,1)S(1)} %collective-permute-done.20.refs_1_, bf16[24,1024]{1,0:T(8,128)(2,1)S(1)} %collective-permute-done.21.refs_2_, ...), custom_call_target="tpu_custom_call" | custom-call | flops 6442450944 | bytes 36700160 | tf_op jit(solution)/shard_map/back/pallas_call | solution.py:168
  124.0 1.7 fold.4
  126.7 1.6 collective-permute-start.37
  131.0 2.5 %collective-permute-done.38.refs_7_ = bf16[24,1024]{1,0:T(8,128)(2,1)S(1)} collective-permute-done((bf16[24,1024]{1,0:T(8,128)(2,1)}, bf16[24,1024]{1,0:T(8,128)(2,1)S(1)}, u32[]{:S(2)}, u32[]{:S(2)}) %collective-permute-start.38) | collective-permute-done | bytes 49184 | tf_op jit(solution)/shard_map/ppermute | solution.py:28
  134.2 1.8 finish.4
  136.0 1.8 collective-permute-start.39
  137.8 3.6 %collective-permute-start.40 = (bf16[24,1024]{1,0:T(8,128)(2,1)}, bf16[24,1024]{1,0:T(8,128)(2,1)S(1)}, u32[]{:S(2)}, u32[]{:S(2)}) collective-permute-start(bf16[24,1024]{1,0:T(8,128)(2,1)} %get-tuple-element.44), channel_id=1, source_target_pairs={{10,0},{11,1},{8,2},{9,3},{14,4},{15,5},{12,6},{13,7},{18,8},{19,9... | collective-permute-start | bytes 147464 | tf_op jit(solution)/shard_map/ppermute | solution.py:43
  143.4 3.1 %collective-permute-done.41.refs_2_ = bf16[24,1024]{1,0:T(8,128)(2,1)S(1)} collective-permute-done((bf16[24,1024]{1,0:T(8,128)(2,1)}, bf16[24,1024]{1,0:T(8,128)(2,1)S(1)}, u32[]{:S(2)}, u32[]{:S(2)}) %collective-permute-start.41) | collective-permute-done | bytes 49184 | tf_op jit(solution)/shard_map/ppermute | solution.py:43
  147.5 5.8 %copy-done.2 = bf16[1,1024,8192]{2,1,0:T(8,128)(2,1)S(1)} copy-done((bf16[1,1024,8192]{2,1,0:T(8,128)(2,1)S(1)}, bf16[1,1024,8192]{2,1,0:T(8,128)(2,1)}, u32[]{:S(2)}) %copy-start.2) | copy-done | bytes 16777240
  153.3 5.7 %gate.5.refs_8_ = bf16[8192,192]{1,0:T(8,128)(2,1)S(1)} custom-call(bf16[24,1024]{1,0:T(8,128)(2,1)S(1)} %get-tuple-element.67.refs_0_.refs_2_, bf16[24,1024]{1,0:T(8,128)(2,1)S(1)} %get-tuple-element.65.refs_1_, bf16[24,1024]{1,0:T(8,128)(2,1)S(1)} %get-tuple-element.63.refs_2_, bf16[24,1024]{1,0:T(8,128)(2,1)S(1)} %get-tuple-element.61.refs_3_, ...), custom_call_target="tpu_custom_call" | custom-call | flops 3221225472 | bytes 19922944 | tf_op jit(solution)/shard_map/gate/pallas_call | solution.py:108
  159.1 22.9 %back.5 = (f32[96,1024]{1,0:T(8,128)S(1)}, bf16[96,1024]{1,0:T(8,128)(2,1)S(1)}) custom-call(bf16[24,1024]{1,0:T(8,128)(2,1)S(1)} %collective-permute-done.39.refs_0_.refs_1_, bf16[24,1024]{1,0:T(8,128)(2,1)S(1)} %collective-permute-done.40.refs_1_, bf16[24,1024]{1,0:T(8,128)(2,1)S(1)} %collective-permute-done.41.refs_2_, ...), custom_call_target="tpu_custom_call" | custom-call | flops 6442450944 | bytes 36700160 | tf_op jit(solution)/shard_map/back/pallas_call | solution.py:168
  184.9 1.7 fold.5
  192.4 1.9 collective-permute-done.50.refs_9_
  194.9 1.9 finish.5
  (146 shorter events, 41.2 us)
Async XLA Ops:
  1.6 7.4 %collective-permute-start.7 = (bf16[24,1024]{1,0:T(8,128)(2,1)}, bf16[24,1024]{1,0:T(8,128)(2,1)S(1)}, u32[]{:S(2)}, u32[]{:S(2)}) collective-permute-start(bf16[24,1024]{1,0:T(8,128)(2,1)} %get-tuple-element.29), channel_id=1, source_target_pairs={{0,16},{8,24},{16,0},{24,8},{1,17},{9,25},{17,1},{25,9},{2,18},{10... | collective-permute-start | bytes 147464 | tf_op jit(solution)/shard_map/ppermute | solution.py:33
  5.7 6.0 %collective-permute-start = (bf16[24,1024]{1,0:T(8,128)(2,1)}, bf16[24,1024]{1,0:T(8,128)(2,1)S(1)}, u32[]{:S(2)}, u32[]{:S(2)}) collective-permute-start(bf16[24,1024]{1,0:T(8,128)(2,1)} %bitcast.45), channel_id=1, source_target_pairs={{0,2},{1,3},{2,0},{3,1},{4,6},{5,7},{6,4},{7,5},{8,10},{9,11},{10,... | collective-permute-start | bytes 147464 | tf_op jit(solution)/shard_map/ppermute | solution.py:28
  7.1 7.1 %collective-permute-start.1 = (bf16[24,1024]{1,0:T(8,128)(2,1)}, bf16[24,1024]{1,0:T(8,128)(2,1)S(1)}, u32[]{:S(2)}, u32[]{:S(2)}) collective-permute-start(bf16[24,1024]{1,0:T(8,128)(2,1)} %bitcast.46), channel_id=1, source_target_pairs={{0,4},{1,5},{2,6},{3,7},{4,0},{5,1},{6,2},{7,3},{8,12},{9,13},{10,... | collective-permute-start | bytes 147464 | tf_op jit(solution)/shard_map/ppermute | solution.py:28
  8.7 8.4 %collective-permute-start.27 = (bf16[2,24,1024]{2,1,0:T(8,128)(2,1)}, bf16[2,24,1024]{2,1,0:T(8,128)(2,1)S(1)}, u32[]{:S(2)}, u32[]{:S(2)}) collective-permute-start(bf16[2,24,1024]{2,1,0:T(8,128)(2,1)} %get-tuple-element.37), channel_id=1, source_target_pairs={{0,16},{8,24},{16,0},{24,8},{1,17},{9,25},{17,1},{25,9},{2,18},{10... | collective-permute-start | bytes 294920 | tf_op jit(solution)/shard_map/ppermute | solution.py:33
  9.0 7.1 %collective-permute-start.8 = (bf16[24,1024]{1,0:T(8,128)(2,1)S(1)}, bf16[24,1024]{1,0:T(8,128)(2,1)S(1)}, u32[]{:S(2)}, u32[]{:S(2)}) collective-permute-start(bf16[24,1024]{1,0:T(8,128)(2,1)S(1)} %collective-permute-done.7.refs_0_.refs_2_), channel_id=1, source_target_pairs={{0,2},{1,3},{2,0},{3,1},{4,6},{5,7},{6,4},{7,5},{8,10},{9,11},{10,... | collective-permute-start | bytes 147464 | tf_op jit(solution)/shard_map/ppermute | solution.py:28
  10.2 5.9 %collective-permute-start.9 = (bf16[24,1024]{1,0:T(8,128)(2,1)S(1)}, bf16[24,1024]{1,0:T(8,128)(2,1)S(1)}, u32[]{:S(2)}, u32[]{:S(2)}) collective-permute-start(bf16[24,1024]{1,0:T(8,128)(2,1)S(1)} %collective-permute-done.7.refs_0_.refs_2_), channel_id=1, source_target_pairs={{0,4},{1,5},{2,6},{3,7},{4,0},{5,1},{6,2},{7,3},{8,12},{9,13},{10,... | collective-permute-start | bytes 147464 | tf_op jit(solution)/shard_map/ppermute | solution.py:28
  11.7 5.4 %collective-permute-start.10 = (bf16[24,1024]{1,0:T(8,128)(2,1)S(1)}, bf16[24,1024]{1,0:T(8,128)(2,1)S(1)}, u32[]{:S(2)}, u32[]{:S(2)}) collective-permute-start(bf16[24,1024]{1,0:T(8,128)(2,1)S(1)} %collective-permute-done.7.refs_0_.refs_2_), channel_id=1, source_target_pairs={{0,6},{1,7},{2,4},{3,5},{4,2},{5,3},{6,0},{7,1},{8,14},{9,15},{10,... | collective-permute-start | bytes 147464 | tf_op jit(solution)/shard_map/ppermute | solution.py:28
  14.3 5.2 %collective-permute-start.2 = (bf16[24,1024]{1,0:T(8,128)(2,1)}, bf16[24,1024]{1,0:T(8,128)(2,1)S(1)}, u32[]{:S(2)}, u32[]{:S(2)}) collective-permute-start(bf16[24,1024]{1,0:T(8,128)(2,1)} %bitcast.47), channel_id=1, source_target_pairs={{0,6},{1,7},{2,4},{3,5},{4,2},{5,3},{6,0},{7,1},{8,14},{9,15},{10,... | collective-permute-start | bytes 147464 | tf_op jit(solution)/shard_map/ppermute | solution.py:28
  19.5 15.0 %collective-permute-start.3 = (bf16[24,1024]{1,0:T(8,128)(2,1)}, bf16[24,1024]{1,0:T(8,128)(2,1)S(1)}, u32[]{:S(2)}, u32[]{:S(2)}) collective-permute-start(bf16[24,1024]{1,0:T(8,128)(2,1)} %bitcast.48), channel_id=1, source_target_pairs={{0,1},{1,0},{2,3},{3,2},{4,5},{5,4},{6,7},{7,6},{8,9},{9,8},{10,11... | collective-permute-start | bytes 147464 | tf_op jit(solution)/shard_map/ppermute | solution.py:28
  19.5 15.6 %collective-permute-start.4 = (bf16[24,1024]{1,0:T(8,128)(2,1)S(1)}, bf16[24,1024]{1,0:T(8,128)(2,1)S(1)}, u32[]{:S(2)}, u32[]{:S(2)}) collective-permute-start(bf16[24,1024]{1,0:T(8,128)(2,1)S(1)} %collective-permute-done.refs_1_), channel_id=1, source_target_pairs={{0,1},{1,0},{2,3},{3,2},{4,5},{5,4},{6,7},{7,6},{8,9},{9,8},{10,11... | collective-permute-start | bytes 147464 | tf_op jit(solution)/shard_map/ppermute | solution.py:28
  20.0 16.3 %collective-permute-start.5 = (bf16[24,1024]{1,0:T(8,128)(2,1)S(1)}, bf16[24,1024]{1,0:T(8,128)(2,1)S(1)}, u32[]{:S(2)}, u32[]{:S(2)}) collective-permute-start(bf16[24,1024]{1,0:T(8,128)(2,1)S(1)} %collective-permute-done.1.refs_2_), channel_id=1, source_target_pairs={{0,1},{1,0},{2,3},{3,2},{4,5},{5,4},{6,7},{7,6},{8,9},{9,8},{10,11... | collective-permute-start | bytes 147464 | tf_op jit(solution)/shard_map/ppermute | solution.py:28
  20.1 16.2 %collective-permute-start.6 = (bf16[24,1024]{1,0:T(8,128)(2,1)S(1)}, bf16[24,1024]{1,0:T(8,128)(2,1)S(1)}, u32[]{:S(2)}, u32[]{:S(2)}) collective-permute-start(bf16[24,1024]{1,0:T(8,128)(2,1)S(1)} %collective-permute-done.2.refs_3_), channel_id=1, source_target_pairs={{0,1},{1,0},{2,3},{3,2},{4,5},{5,4},{6,7},{7,6},{8,9},{9,8},{10,11... | collective-permute-start | bytes 147464 | tf_op jit(solution)/shard_map/ppermute | solution.py:28
  20.5 39.9 %collective-permute-start.30 = (bf16[2,24,1024]{2,1,0:T(8,128)(2,1)S(1)}, bf16[2,24,1024]{2,1,0:T(8,128)(2,1)S(1)}, u32[]{:S(2)}, u32[]{:S(2)}) collective-permute-start(bf16[2,24,1024]{2,1,0:T(8,128)(2,1)S(1)} %collective-permute-done.27), channel_id=1, source_target_pairs={{0,6},{1,7},{2,4},{3,5},{4,2},{5,3},{6,0},{7,1},{8,14},{9,15},{10,... | collective-permute-start | bytes 294920 | tf_op jit(solution)/shard_map/ppermute | solution.py:28
  34.5 26.0 %collective-permute-start.29 = (bf16[2,24,1024]{2,1,0:T(8,128)(2,1)S(1)}, bf16[2,24,1024]{2,1,0:T(8,128)(2,1)S(1)}, u32[]{:S(2)}, u32[]{:S(2)}) collective-permute-start(bf16[2,24,1024]{2,1,0:T(8,128)(2,1)S(1)} %collective-permute-done.27), channel_id=1, source_target_pairs={{0,4},{1,5},{2,6},{3,7},{4,0},{5,1},{6,2},{7,3},{8,12},{9,13},{10,... | collective-permute-start | bytes 294920 | tf_op jit(solution)/shard_map/ppermute | solution.py:28
  35.1 26.0 %collective-permute-start.28 = (bf16[2,24,1024]{2,1,0:T(8,128)(2,1)S(1)}, bf16[2,24,1024]{2,1,0:T(8,128)(2,1)S(1)}, u32[]{:S(2)}, u32[]{:S(2)}) collective-permute-start(bf16[2,24,1024]{2,1,0:T(8,128)(2,1)S(1)} %collective-permute-done.27), channel_id=1, source_target_pairs={{0,2},{1,3},{2,0},{3,1},{4,6},{5,7},{6,4},{7,5},{8,10},{9,11},{10,... | collective-permute-start | bytes 294920 | tf_op jit(solution)/shard_map/ppermute | solution.py:28
  36.3 24.9 %collective-permute-start.31 = (bf16[2,24,1024]{2,1,0:T(8,128)(2,1)S(1)}, bf16[2,24,1024]{2,1,0:T(8,128)(2,1)S(1)}, u32[]{:S(2)}, u32[]{:S(2)}) collective-permute-start(bf16[2,24,1024]{2,1,0:T(8,128)(2,1)S(1)} %collective-permute-done.27), channel_id=1, source_target_pairs={{0,1},{1,0},{2,3},{3,2},{4,5},{5,4},{6,7},{7,6},{8,9},{9,8},{10,11... | collective-permute-start | bytes 294920 | tf_op jit(solution)/shard_map/ppermute | solution.py:28
  60.5 7.2 %collective-permute-start.33 = (bf16[2,24,1024]{2,1,0:T(8,128)(2,1)S(1)}, bf16[2,24,1024]{2,1,0:T(8,128)(2,1)S(1)}, u32[]{:S(2)}, u32[]{:S(2)}) collective-permute-start(bf16[2,24,1024]{2,1,0:T(8,128)(2,1)S(1)} %collective-permute-done.29), channel_id=1, source_target_pairs={{0,1},{1,0},{2,3},{3,2},{4,5},{5,4},{6,7},{7,6},{8,9},{9,8},{10,11... | collective-permute-start | bytes 294920 | tf_op jit(solution)/shard_map/ppermute | solution.py:28
  61.1 20.9 %collective-permute-start.32 = (bf16[2,24,1024]{2,1,0:T(8,128)(2,1)S(1)}, bf16[2,24,1024]{2,1,0:T(8,128)(2,1)S(1)}, u32[]{:S(2)}, u32[]{:S(2)}) collective-permute-start(bf16[2,24,1024]{2,1,0:T(8,128)(2,1)S(1)} %collective-permute-done.28), channel_id=1, source_target_pairs={{0,1},{1,0},{2,3},{3,2},{4,5},{5,4},{6,7},{7,6},{8,9},{9,8},{10,11... | collective-permute-start | bytes 294920 | tf_op jit(solution)/shard_map/ppermute | solution.py:28
  74.2 7.8 %collective-permute-start.19 = (bf16[24,1024]{1,0:T(8,128)(2,1)}, bf16[24,1024]{1,0:T(8,128)(2,1)S(1)}, u32[]{:S(2)}, u32[]{:S(2)}) collective-permute-start(bf16[24,1024]{1,0:T(8,128)(2,1)} %get-tuple-element.36), channel_id=1, source_target_pairs={{8,0},{9,1},{10,2},{11,3},{12,4},{13,5},{14,6},{15,7},{16,8},{17,9... | collective-permute-start | bytes 147464 | tf_op jit(solution)/shard_map/ppermute | solution.py:43
  79.9 5.2 %collective-permute-start.20 = (bf16[24,1024]{1,0:T(8,128)(2,1)}, bf16[24,1024]{1,0:T(8,128)(2,1)S(1)}, u32[]{:S(2)}, u32[]{:S(2)}) collective-permute-start(bf16[24,1024]{1,0:T(8,128)(2,1)} %get-tuple-element.36), channel_id=1, source_target_pairs={{10,0},{11,1},{8,2},{9,3},{14,4},{15,5},{12,6},{13,7},{18,8},{19,9... | collective-permute-start | bytes 147464 | tf_op jit(solution)/shard_map/ppermute | solution.py:43
  80.4 6.2 %collective-permute-start.22 = (bf16[24,1024]{1,0:T(8,128)(2,1)}, bf16[24,1024]{1,0:T(8,128)(2,1)S(1)}, u32[]{:S(2)}, u32[]{:S(2)}) collective-permute-start(bf16[24,1024]{1,0:T(8,128)(2,1)} %get-tuple-element.36), channel_id=1, source_target_pairs={{14,0},{15,1},{12,2},{13,3},{10,4},{11,5},{8,6},{9,7},{22,8},{23,9... | collective-permute-start | bytes 147464 | tf_op jit(solution)/shard_map/ppermute | solution.py:43
  82.0 16.1 %collective-permute-start.23 = (bf16[24,1024]{1,0:T(8,128)(2,1)S(1)}, bf16[24,1024]{1,0:T(8,128)(2,1)S(1)}, u32[]{:S(2)}, u32[]{:S(2)}) collective-permute-start(bf16[24,1024]{1,0:T(8,128)(2,1)S(1)} %collective-permute-done.19.refs_0_.refs_1_), channel_id=1, source_target_pairs={{0,1},{1,0},{2,3},{3,2},{4,5},{5,4},{6,7},{7,6},{8,9},{9,8},{10,11... | collective-permute-start | bytes 147464 | tf_op jit(solution)/shard_map/ppermute | solution.py:28
  85.1 13.0 %collective-permute-start.24 = (bf16[24,1024]{1,0:T(8,128)(2,1)S(1)}, bf16[24,1024]{1,0:T(8,128)(2,1)S(1)}, u32[]{:S(2)}, u32[]{:S(2)}) collective-permute-start(bf16[24,1024]{1,0:T(8,128)(2,1)S(1)} %collective-permute-done.20.refs_1_), channel_id=1, source_target_pairs={{0,1},{1,0},{2,3},{3,2},{4,5},{5,4},{6,7},{7,6},{8,9},{9,8},{10,11... | collective-permute-start | bytes 147464 | tf_op jit(solution)/shard_map/ppermute | solution.py:28
  85.5 12.5 %collective-permute-start.25 = (bf16[24,1024]{1,0:T(8,128)(2,1)S(1)}, bf16[24,1024]{1,0:T(8,128)(2,1)S(1)}, u32[]{:S(2)}, u32[]{:S(2)}) collective-permute-start(bf16[24,1024]{1,0:T(8,128)(2,1)S(1)} %collective-permute-done.21.refs_2_), channel_id=1, source_target_pairs={{0,1},{1,0},{2,3},{3,2},{4,5},{5,4},{6,7},{7,6},{8,9},{9,8},{10,11... | collective-permute-start | bytes 147464 | tf_op jit(solution)/shard_map/ppermute | solution.py:28
  86.6 11.5 %collective-permute-start.26 = (bf16[24,1024]{1,0:T(8,128)(2,1)S(1)}, bf16[24,1024]{1,0:T(8,128)(2,1)S(1)}, u32[]{:S(2)}, u32[]{:S(2)}) collective-permute-start(bf16[24,1024]{1,0:T(8,128)(2,1)S(1)} %collective-permute-done.22.refs_3_), channel_id=1, source_target_pairs={{0,1},{1,0},{2,3},{3,2},{4,5},{5,4},{6,7},{7,6},{8,9},{9,8},{10,11... | collective-permute-start | bytes 147464 | tf_op jit(solution)/shard_map/ppermute | solution.py:28
  136.0 6.9 %collective-permute-start.39 = (bf16[24,1024]{1,0:T(8,128)(2,1)}, bf16[24,1024]{1,0:T(8,128)(2,1)S(1)}, u32[]{:S(2)}, u32[]{:S(2)}) collective-permute-start(bf16[24,1024]{1,0:T(8,128)(2,1)} %get-tuple-element.44), channel_id=1, source_target_pairs={{8,0},{9,1},{10,2},{11,3},{12,4},{13,5},{14,6},{15,7},{16,8},{17,9... | collective-permute-start | bytes 147464 | tf_op jit(solution)/shard_map/ppermute | solution.py:43
  137.8 5.6 %collective-permute-start.40 = (bf16[24,1024]{1,0:T(8,128)(2,1)}, bf16[24,1024]{1,0:T(8,128)(2,1)S(1)}, u32[]{:S(2)}, u32[]{:S(2)}) collective-permute-start(bf16[24,1024]{1,0:T(8,128)(2,1)} %get-tuple-element.44), channel_id=1, source_target_pairs={{10,0},{11,1},{8,2},{9,3},{14,4},{15,5},{12,6},{13,7},{18,8},{19,9... | collective-permute-start | bytes 147464 | tf_op jit(solution)/shard_map/ppermute | solution.py:43
  141.4 6.1 %collective-permute-start.42 = (bf16[24,1024]{1,0:T(8,128)(2,1)}, bf16[24,1024]{1,0:T(8,128)(2,1)S(1)}, u32[]{:S(2)}, u32[]{:S(2)}) collective-permute-start(bf16[24,1024]{1,0:T(8,128)(2,1)} %get-tuple-element.44), channel_id=1, source_target_pairs={{14,0},{15,1},{12,2},{13,3},{10,4},{11,5},{8,6},{9,7},{22,8},{23,9... | collective-permute-start | bytes 147464 | tf_op jit(solution)/shard_map/ppermute | solution.py:43
  142.9 16.1 %collective-permute-start.43 = (bf16[24,1024]{1,0:T(8,128)(2,1)S(1)}, bf16[24,1024]{1,0:T(8,128)(2,1)S(1)}, u32[]{:S(2)}, u32[]{:S(2)}) collective-permute-start(bf16[24,1024]{1,0:T(8,128)(2,1)S(1)} %collective-permute-done.39.refs_0_.refs_1_), channel_id=1, source_target_pairs={{0,1},{1,0},{2,3},{3,2},{4,5},{5,4},{6,7},{7,6},{8,9},{9,8},{10,11... | collective-permute-start | bytes 147464 | tf_op jit(solution)/shard_map/ppermute | solution.py:28
  143.4 15.6 %collective-permute-start.44 = (bf16[24,1024]{1,0:T(8,128)(2,1)S(1)}, bf16[24,1024]{1,0:T(8,128)(2,1)S(1)}, u32[]{:S(2)}, u32[]{:S(2)}) collective-permute-start(bf16[24,1024]{1,0:T(8,128)(2,1)S(1)} %collective-permute-done.40.refs_1_), channel_id=1, source_target_pairs={{0,1},{1,0},{2,3},{3,2},{4,5},{5,4},{6,7},{7,6},{8,9},{9,8},{10,11... | collective-permute-start | bytes 147464 | tf_op jit(solution)/shard_map/ppermute | solution.py:28
  146.5 12.5 %collective-permute-start.45 = (bf16[24,1024]{1,0:T(8,128)(2,1)S(1)}, bf16[24,1024]{1,0:T(8,128)(2,1)S(1)}, u32[]{:S(2)}, u32[]{:S(2)}) collective-permute-start(bf16[24,1024]{1,0:T(8,128)(2,1)S(1)} %collective-permute-done.41.refs_2_), channel_id=1, source_target_pairs={{0,1},{1,0},{2,3},{3,2},{4,5},{5,4},{6,7},{7,6},{8,9},{9,8},{10,11... | collective-permute-start | bytes 147464 | tf_op jit(solution)/shard_map/ppermute | solution.py:28
  147.5 11.5 %collective-permute-start.46 = (bf16[24,1024]{1,0:T(8,128)(2,1)S(1)}, bf16[24,1024]{1,0:T(8,128)(2,1)S(1)}, u32[]{:S(2)}, u32[]{:S(2)}) collective-permute-start(bf16[24,1024]{1,0:T(8,128)(2,1)S(1)} %collective-permute-done.42.refs_3_), channel_id=1, source_target_pairs={{0,1},{1,0},{2,3},{3,2},{4,5},{5,4},{6,7},{7,6},{8,9},{9,8},{10,11... | collective-permute-start | bytes 147464 | tf_op jit(solution)/shard_map/ppermute | solution.py:28
  (46 other events, 476.9 us)
